TPU v7x, 32 devices: a whole 2x2x4 slice. The times are simulated.
32 devices in a mesh: row: 2 (over x), col: 2 (over y), dp: 8 (over z, core).
Axes of the slice: x: 2, y: 2, z: 4, core: 2. Of those that a mesh axis runs over, the one named last changes fastest.
Arguments:
- features: bfloat16 [8, 48, 48, 1024], P('dp', 'row', 'col'), may hold values from -6 to 6
- cotangent: bfloat16 [8, 48, 48, 256], P('dp', 'row', 'col'), may hold values from -0.09375 to 0.09375
- w_point: bfloat16 [1024, 256], replicated, may hold values from -0.1875 to 0.1875
- w_rate_a: bfloat16 [3, 3, 1024, 256], replicated, may hold values from -0.0625 to 0.0625
- w_rate_b: bfloat16 [3, 3, 1024, 256], replicated, may hold values from -0.0625 to 0.0625
- w_rate_c: bfloat16 [3, 3, 1024, 256], replicated, may hold values from -0.0625 to 0.0625
- w_proj: bfloat16 [1024, 256], replicated, may hold values from -0.1875 to 0.1875
- bucket_slot: int32 [176], replicated, may hold values from 0 to 183, as said below
Outputs:
- owned_grads: float32 [184, 16384], P('dp', ('row', 'col'))
Inputs may be any that keep to these rules, and one draw needn't show every extreme that they name: Distinct slot numbers, one for each of the 176 slices; slice s belongs to data replica bucket_slot[s] // 23. In every draw all 23 slots of some replica are taken. Rows of owned_grads that no slice names are zero.
All inputs are finite; a program needn't handle non-finite values.
Results may differ from a plain program's by a relative error of at most 0.0043.
Values may be sent and summed in bfloat16 or wider, within the bound.
A program may use at most 192 MiB of HBM per device.

v0:
```python
import jax
import jax.numpy as jnp
from jax import lax
from jax.sharding import PartitionSpec as P

RATE_A = 6
RATE_B = 12
RATE_C = 18
SROWS = 64


def extended(cells, sides, width):
    for axis, dim in sides:
        count = lax.axis_size(axis)
        ends = count - 1
        head = lax.slice_in_dim(cells, 0, width, axis=dim)
        tail = lax.slice_in_dim(cells, cells.shape[dim] - width, cells.shape[dim], axis=dim)
        cells = jnp.concatenate(
            [
                lax.ppermute(tail, axis, [(i, (i + 1) % count) for i in range(ends)]),
                cells,
                lax.ppermute(head, axis, [((i + 1) % count, i) for i in range(ends)]),
            ],
            axis=dim,
        )
    return cells


def silu_slope(value):
    sig = jax.nn.sigmoid(value)
    return sig * (1.0 + value * (1.0 - sig))


def contract_pixels(left, right):
    return lax.dot_general(
        left, right, (((0,), (0,)), ((), ())), preferred_element_type=jnp.float32
    )


def shards(features, cotangent, w_point, w_rate_a, w_rate_b, w_rate_c, w_proj, bucket_slot):
    image = features[0]
    rows_dev, cols_dev, chans = image.shape
    out_width = w_point.shape[1]
    pixels = rows_dev * cols_dev
    width = RATE_C
    padded = extended(image, (("row", 0), ("col", 1)), width)

    def window(rate, above, across):
        top = width + above * rate
        left = width + across * rate
        return padded[top : top + rows_dev, left : left + cols_dev].reshape(pixels, chans)

    rates = (RATE_A, RATE_B, RATE_C)
    kernels = (w_rate_a, w_rate_b, w_rate_c)
    centre = window(0, 0, 0)
    pre_list = [jnp.dot(centre, w_point, preferred_element_type=jnp.float32)]
    for rate, kernel in zip(rates, kernels):
        total = jnp.zeros((pixels, out_width), jnp.float32)
        for above in range(3):
            for across in range(3):
                total = total + jnp.dot(
                    window(rate, above - 1, across - 1),
                    kernel[above, across],
                    preferred_element_type=jnp.float32,
                )
        pre_list.append(total)
    joined = jnp.concatenate([jax.nn.silu(pre) for pre in pre_list], 1).astype(jnp.bfloat16)
    proj_pre = jnp.dot(joined, w_proj, preferred_element_type=jnp.float32)
    upstream = cotangent[0].reshape(pixels, out_width).astype(jnp.float32)
    g_proj = (upstream * silu_slope(proj_pre)).astype(jnp.bfloat16)
    pieces = [contract_pixels(joined, g_proj)]
    d_joined = lax.dot_general(
        g_proj, w_proj, (((1,), (1,)), ((), ())), preferred_element_type=jnp.float32
    )
    for index in (0, 3):
        pre = pre_list[index]
        d_pre = (d_joined[:, index * out_width : (index + 1) * out_width] * silu_slope(pre)).astype(
            jnp.bfloat16
        )
        if index == 0:
            pieces.append(contract_pixels(centre, d_pre))
        else:
            for above in range(3):
                for across in range(3):
                    pieces.append(contract_pixels(window(RATE_C, above - 1, across - 1), d_pre))
    stacked = jnp.concatenate(pieces, 0)
    nslice = stacked.shape[0] // SROWS
    slices = stacked.reshape(nslice, SROWS * out_width)
    replicas = lax.axis_size("dp")
    capacity = nslice // replicas + 1
    slot_count = capacity * replicas
    buffer = jnp.zeros((slot_count, slices.shape[1]), jnp.float32).at[bucket_slot].set(slices)
    summed = lax.psum_scatter(buffer, ("row", "col"), scatter_dimension=1, tiled=True)
    result = lax.psum_scatter(summed, "dp", scatter_dimension=0, tiled=True)
    return result


def solution(mesh):
    placed = (
        P("dp", "row", "col", None),
        P("dp", "row", "col", None),
        P(),
        P(),
        P(),
        P(),
        P(),
        P(),
    )
    return jax.shard_map(
        shards, mesh=mesh, in_specs=placed, out_specs=P("dp", ("row", "col")), check_vma=False
    )
```

profile of v0, /device:TPU:1, one launch (start us, length us, event | category | flops | bytes accessed | tf_op | source)
XLA Modules:
  0.0 364.7 jit_solution(4375736542636065797)
XLA Ops:
  6.5 1.7 slice_bitcast_fusion.1
  8.3 4.0 %collective-permute-start = (bf16[18,24,1024]{2,1,0:T(8,128)(2,1)S(1)}, bf16[18,24,1024]{2,1,0:T(8,128)(2,1)S(1)}, u32[]{:S(2)}, u32[]{:S(2)}) collective-permute-start(bf16[18,24,1024]{2,1,0:T(8,128)(2,1)S(1)} %get-tuple-element.36), channel_id=1, source_target_pairs={{0,16},{1,17},{2,18},{3,19},{4,20},{5,21},{6,22},{7,23},{8,24},{9,... | collective-permute-start | bytes 2654216 | tf_op jit(solution)/shard_map/ppermute | solution.py:20
  12.3 1.3 collective-permute-start.1
  13.6 2.4 fusion.62
  15.9 2.3 fusion.45
  18.3 2.4 fusion.28
  20.7 1.3 multiply_convert_fusion.3
  21.9 8.6 %collective-permute-done = bf16[18,24,1024]{2,1,0:T(8,128)(2,1)S(1)} collective-permute-done((bf16[18,24,1024]{2,1,0:T(8,128)(2,1)S(1)}, bf16[18,24,1024]{2,1,0:T(8,128)(2,1)S(1)}, u32[]{:S(2)}, u32[]{:S(2)}) %collective-permute-start) | collective-permute-done | bytes 884768 | tf_op jit(solution)/shard_map/ppermute | solution.py:20
  30.5 3.8 %collective-permute-done.1 = bf16[18,24,1024]{2,1,0:T(8,128)(2,1)S(1)} collective-permute-done((bf16[18,24,1024]{2,1,0:T(8,128)(2,1)S(1)}, bf16[18,24,1024]{2,1,0:T(8,128)(2,1)S(1)}, u32[]{:S(2)}, u32[]{:S(2)}) %collective-permute-start.1) | collective-permute-done | bytes 884768 | tf_op jit(solution)/shard_map/ppermute | solution.py:22
  34.7 1.8 fusion.107
  36.5 1.2 copy.18
  37.7 3.3 collective-permute-start.2
  41.0 1.2 copy.20
  42.3 1.5 collective-permute-start.3
  43.8 0.7 fusion.17
  44.5 2.8 fusion.57
  47.2 2.4 fusion.68
  49.6 2.3 fusion.40
  52.0 2.3 fusion.51
  54.3 2.4 fusion.23
  56.7 2.3 fusion.34
  59.0 30.5 %collective-permute-done.2 = bf16[60,18,1024]{2,0,1:T(8,128)(2,1)S(1)} collective-permute-done((bf16[60,18,1024]{2,0,1:T(8,128)(2,1)S(1)}, bf16[60,18,1024]{2,0,1:T(8,128)(2,1)S(1)}, u32[]{:S(2)}, u32[]{:S(2)}) %collective-permute-start.2) | collective-permute-done | bytes 2211872 | tf_op jit(solution)/shard_map/ppermute | solution.py:20
  89.5 1.3 copy.19
  90.8 3.9 %collective-permute-done.3 = bf16[60,18,1024]{2,0,1:T(8,128)(2,1)S(1)} collective-permute-done((bf16[60,18,1024]{2,0,1:T(8,128)(2,1)S(1)}, bf16[60,18,1024]{2,0,1:T(8,128)(2,1)S(1)}, u32[]{:S(2)}, u32[]{:S(2)}) %collective-permute-start.3) | collective-permute-done | bytes 2211872 | tf_op jit(solution)/shard_map/ppermute | solution.py:22
  94.8 1.3 copy.21
  96.0 4.9 %maximum_maximum_fusion = (bf16[60,42,1024]{2,1,0:T(8,128)(2,1)S(1)}, bf16[60,42,1024]{2,1,0:T(8,128)(2,1)}) fusion(bf16[18,24,1024]{2,1,0:T(8,128)(2,1)S(1)} %collective-permute-done.1, bf16[24,24,1024]{2,1,0:T(8,128)(2,1)S(1)} %bitcast.185, bf16[18,24,1024]{2,1,0:T(8,128)(2,1)S(1)} %collective-permute-done, bf16[60,18,1024]{2,1,0:T(8,128)(2,1)S(1)} %copy.19, ...), kind=kLoop, calls=%fused_computation.3 | loop fusion | flops 41287680 | bytes 17694720 | tf_op jit(solution)/shard_map/concatenate | solution.py:18
  100.9 14.8 %fusion.105 = (bf16[24,24,1024]{2,1,0:T(8,128)(2,1)}, bf16[24,24,1024]{2,1,0:T(8,128)(2,1)}, bf16[24,24,1024]{2,1,0:T(8,128)(2,1)}, bf16[24,24,1024]{2,1,0:T(8,1...) fusion(bf16[60,42,1024]{2,1,0:T(8,128)(2,1)S(1)} %get-tuple-ele, ...), kind=kLoop, calls=%fused_computation.145 | loop fusion | bytes 42467328 | tf_op jit(solution)/shard_map/slice | solution.py:51
  115.7 2.0 fusion.55
  117.7 1.6 fusion.59
  119.3 1.6 fusion.64
  121.0 1.6 fusion.66
  122.6 1.6 fusion.70
  124.3 1.6 fusion.38
  125.9 1.6 fusion.42
  127.5 1.6 fusion.47
  129.2 1.6 fusion.49
  130.8 1.6 fusion.53
  132.4 1.6 fusion.21
  134.1 1.6 fusion.25
  135.7 1.6 fusion.30
  137.4 1.7 fusion.32
  139.1 1.6 fusion.36
  140.8 1.9 multiply_convert_fusion.2
  142.8 1.9 multiply_convert_fusion.1
  144.7 1.7 multiply_convert_fusion
  147.6 1.6 convolution_dynamic-update-slice_fusion.8
  149.4 1.0 copy-done.3
  150.4 1.8 fusion.4
  152.3 1.6 convolution_dynamic-update-slice_fusion.7
  153.9 1.6 convolution_dynamic-update-slice_fusion.6
  155.5 1.7 convolution_dynamic-update-slice_fusion.5
  157.2 1.9 convolution_dynamic-update-slice_fusion.4
  159.1 1.7 fusion.3
  160.8 1.6 convolution_dynamic-update-slice_fusion.3
  162.4 1.6 convolution_dynamic-update-slice_fusion.2
  164.0 1.6 convolution_dynamic-update-slice_fusion.1
  165.6 1.6 convolution_dynamic-update-slice_fusion
  167.2 13.5 %reshape.117 = f32[176,16384]{1,0:T(8,128)} reshape(f32[11264,256]{1,0:T(8,128)} %convolution_dynamic-update-slice_fusion) | data formatting | bytes 23068672 | tf_op jit(solution)/shard_map/reshape | solution.py:88
  180.7 15.5 %scatter_custom_fusion = f32[184,16384]{1,0:T(8,128)} fusion(s32[176]{0:T(256)S(1)} %compare_select_fusion, f32[176,16384]{1,0:T(8,128)} %reshape.117, f32[]{:T(128)} %constant.4.clone.1), kind=kCustom, calls=%fused_computation.1 | custom fusion | bytes 12059136 | tf_op jit(solution)/shard_map/scatter | solution.py:92
  196.3 118.3 %reduce-scatter.4.cloned.1.call-done = f32[184,4096]{1,0:T(8,128)} async-done(((f32[184,16384]{1,0:T(8,128)}), f32[184,4096]{1,0:T(8,128)}) %reduce-scatter.4.cloned.1.call-update) | async-done | bytes 3014672 | tf_op jit(solution)/shard_map/reduce_scatter | solution.py:93
  314.6 34.9 %fusion = f32[24,4096]{1,0:T(8,128)S(1)} fusion(f32[184,4096]{1,0:T(8,128)} %reduce-scatter.4.cloned.1.call-done), kind=kCustom, calls=%all-reduce-scatter | all-reduce-scatter fusion | flops 786433 | bytes 3408384
  349.5 4.3 %collective-permute-start.4 = (f32[7,4096]{1,0:T(8,128)S(1)}, f32[7,4096]{1,0:T(8,128)S(1)}, u32[]{:S(2)}, u32[]{:S(2)}) collective-permute-start(f32[7,4096]{1,0:T(8,128)S(1)} %slice.298), channel_id=1, source_target_pairs={{0,1},{1,2},{2,3},{3,4},{4,5},{5,6},{6,7},{8,9},{9,10},{10,11},{11... | collective-permute-start | bytes 344072
  355.1 1.2 collective-permute-done.4
  356.6 0.8 constant_dynamic-slice_fusion
  (87 shorter events, 2.8 us)
Async XLA Ops:
  6.5 139.9 %copy-start = (bf16[1024,256]{1,0:T(8,128)(2,1)S(1)}, bf16[1024,256]{1,0:T(8,128)(2,1)}, u32[]{:S(2)}) copy-start(bf16[1024,256]{1,0:T(8,128)(2,1)} %param.14) | copy-start | bytes 1572868
  6.5 7.0 %copy-start.1 = (bf16[1,24,24,1024]{3,2,1,0:T(8,128)(2,1)S(1)}, bf16[1,24,24,1024]{3,2,1,0:T(8,128)(2,1)}, u32[]{:S(2)}) copy-start(bf16[1,24,24,1024]{3,2,1,0:T(8,128)(2,1)} %param.8) | copy-start | bytes 3538948
  6.5 308.1 %reduce-scatter.4.cloned.1.call-start = ((), (), s32[]{:S(2)}) async-start(), calls=%async_computation.1 | async-start | bytes 15073280 | tf_op jit(solution)/shard_map/reduce_scatter | solution.py:93
  8.3 22.3 %collective-permute-start = (bf16[18,24,1024]{2,1,0:T(8,128)(2,1)S(1)}, bf16[18,24,1024]{2,1,0:T(8,128)(2,1)S(1)}, u32[]{:S(2)}, u32[]{:S(2)}) collective-permute-start(bf16[18,24,1024]{2,1,0:T(8,128)(2,1)S(1)} %get-tuple-element.36), channel_id=1, source_target_pairs={{0,16},{1,17},{2,18},{3,19},{4,20},{5,21},{6,22},{7,23},{8,24},{9,... | collective-permute-start | bytes 2654216 | tf_op jit(solution)/shard_map/ppermute | solution.py:20
  12.3 22.1 %collective-permute-start.1 = (bf16[18,24,1024]{2,1,0:T(8,128)(2,1)S(1)}, bf16[18,24,1024]{2,1,0:T(8,128)(2,1)S(1)}, u32[]{:S(2)}, u32[]{:S(2)}) collective-permute-start(bf16[18,24,1024]{2,1,0:T(8,128)(2,1)S(1)} %get-tuple-element.37), channel_id=1, source_target_pairs={{16,0},{17,1},{18,2},{19,3},{20,4},{21,5},{22,6},{23,7},{24,8},{25... | collective-permute-start | bytes 2654216 | tf_op jit(solution)/shard_map/ppermute | solution.py:22
  18.3 2.4 copy-start.36
  37.7 51.8 %collective-permute-start.2 = (bf16[60,18,1024]{2,0,1:T(8,128)(2,1)S(1)}, bf16[60,18,1024]{2,0,1:T(8,128)(2,1)S(1)}, u32[]{:S(2)}, u32[]{:S(2)}) collective-permute-start(bf16[60,18,1024]{2,0,1:T(8,128)(2,1)S(1)} %copy.18), channel_id=1, source_target_pairs={{0,8},{1,9},{2,10},{3,11},{4,12},{5,13},{6,14},{7,15},{16,24},{17,... | collective-permute-start | bytes 6635528 | tf_op jit(solution)/shard_map/ppermute | solution.py:20
  41.0 2.7 copy-start.34
  42.3 52.5 %collective-permute-start.3 = (bf16[60,18,1024]{2,0,1:T(8,128)(2,1)S(1)}, bf16[60,18,1024]{2,0,1:T(8,128)(2,1)S(1)}, u32[]{:S(2)}, u32[]{:S(2)}) collective-permute-start(bf16[60,18,1024]{2,0,1:T(8,128)(2,1)S(1)} %copy.20), channel_id=1, source_target_pairs={{8,0},{9,1},{10,2},{11,3},{12,4},{13,5},{14,6},{15,7},{24,16},{25,... | collective-permute-start | bytes 6635528 | tf_op jit(solution)/shard_map/ppermute | solution.py:22
  44.4 9.9 %copy-start.7 = (bf16[24,24,1024]{2,1,0:T(8,128)(2,1)}, bf16[24,24,1024]{2,1,0:T(8,128)(2,1)S(1)}, u32[]{:S(2)}) copy-start(bf16[24,24,1024]{2,1,0:T(8,128)(2,1)S(1)} %get-tuple-element.34) | copy-start | bytes 3538948
  44.5 12.2 %copy-start.9 = (bf16[24,24,1024]{2,1,0:T(8,128)(2,1)}, bf16[24,24,1024]{2,1,0:T(8,128)(2,1)S(1)}, u32[]{:S(2)}) copy-start(bf16[24,24,1024]{2,1,0:T(8,128)(2,1)S(1)} %get-tuple-element.28) | copy-start | bytes 3538948
  90.8 5.2 %copy-start.2 = (bf16[1,24,24,1024]{3,2,1,0:T(8,128)(2,1)S(1)}, bf16[1,24,24,1024]{3,2,1,0:T(8,128)(2,1)}, u32[]{:S(2)}) copy-start(bf16[1,24,24,1024]{3,2,1,0:T(8,128)(2,1)} %param.8) | copy-start | bytes 3538948
  115.7 2.0 copy-start.24
  117.7 1.6 copy-start.23
  119.3 1.7 copy-start.22
  121.0 1.6 copy-start.21
  122.6 1.6 copy-start.20
  124.2 1.6 copy-start.19
  125.9 1.7 copy-start.18
  127.5 1.6 copy-start.17
  129.1 1.6 copy-start.16
  130.8 1.6 copy-start.11
  132.4 1.7 copy-start.12
  134.1 1.7 copy-start.13
  135.7 1.7 copy-start.14
  137.3 1.7 copy-start.15
  137.4 3.4 copy-start.32
  137.4 3.4 copy-start.33
  139.1 1.7 copy-start.6
  139.1 1.7 copy-start.27
  140.8 1.9 copy-start.5
  140.8 1.9 copy-start.26
  140.8 1.9 copy-start.30
  140.8 1.9 copy-start.31
  142.7 1.9 copy-start.4
  142.7 1.9 copy-start.25
  142.8 1.9 copy-start.28
  142.8 1.9 copy-start.29
  144.7 1.8 copy-start.37
  147.6 1.9 copy-start.38
  149.2 1.3 copy-start.3
  152.3 1.6 copy-start.10
  162.4 1.6 copy-start.8
  196.2 157.6 %copy-start.35 = (u32[32]{0:T(128)S(1)}, u32[32]{0:T(128)}, u32[]{:S(2)}) copy-start(u32[32]{0:T(128)} %constant.17) | copy-start | bytes 388
  349.5 6.7 %collective-permute-start.4 = (f32[7,4096]{1,0:T(8,128)S(1)}, f32[7,4096]{1,0:T(8,128)S(1)}, u32[]{:S(2)}, u32[]{:S(2)}) collective-permute-start(f32[7,4096]{1,0:T(8,128)S(1)} %slice.298), channel_id=1, source_target_pairs={{0,1},{1,2},{2,3},{3,4},{4,5},{5,6},{6,7},{8,9},{9,10},{10,11},{11... | collective-permute-start | bytes 344072
Sparse Core Ops, SparseCore 0:
  196.4 118.1 reduce-scatter.3
where the time goes:
time: 372 us; the launch traced here: 365 us
  waiting for transfers between devices  166 us (45%)
  matrix products  72.5 us (19%)
  local copies, waits for them, and re-layouts  55.2 us (15%)
  blocking collectives  34.9 us (9%)
  between operations  15.3 us (4%)
  starting transfers between devices  14.3 us (4%)
  other arithmetic  6.11 us (2%)
    reduce_scatter x1, waiting for transfers between devices, shards(): lax.psum_scatter(buffer, ('row', 'col'), scatter_dimension=1, tiled=True)  118 us
    dot_general x27, matrix products, shards(): jnp.dot(window(rate, above - 1, across - 1), kernel[above, across], prefe...  51.7 us
    ppermute x2, waiting for transfers between devices, extended(): lax.ppermute(tail, axis, [(i, (i + 1) % count) for i in range(ends)])  39.1 us
    unnamed x1, blocking collectives  34.9 us
    dot_general x11, matrix products, contract_pixels(): lax.dot_general(left, right, (((0,), (0,)), ((), ())), preferred_element_...  18.4 us
    scatter x1, local copies, waits for them, and re-layouts, shards(): jnp.zeros((slot_count, slices.shape[1]), jnp.float32).at[bucket_slot]  15.5 us
    slice x1, local copies, waits for them, and re-layouts, window(): padded[top:top + rows_dev, left:left + cols_dev].reshape(pixels, chans)  14.8 us
    reshape x1, local copies, waits for them, and re-layouts, shards(): slices = stacked.reshape(nslice, SROWS * out_width)  13.5 us
  transfers between devices with their start and end apart: 6, of which 6 were waited for; matrix products, arithmetic and copies ran while one was open for 7% of the time, Pallas kernels for 0%

commit v1 on v0

v1 whole, which is shorter than its diff:
```python
import functools

import jax
import jax.numpy as jnp
from jax import lax
from jax.experimental import pallas as pl
from jax.experimental.pallas import tpu as pltpu
from jax.sharding import PartitionSpec as P

RATES = (18, 12, 6)
SPAN = {18: 0, 12: 18, 6: 30}
DIAG = {18: (0, 0), 12: (18, 0), 6: (0, 18)}
REACH = 18
SROWS = 64
MESH = pl.DeviceIdType.MESH
VMEM = pltpu.VMEM
BF16 = jnp.bfloat16
F32 = jnp.float32
LIMIT = 56 * 1024 * 1024


def silu_slope(value):
    sig = jax.nn.sigmoid(value)
    return sig * (1.0 + value * (1.0 - sig))


def forward_kernel(n, f_ref, wc_ref, wb_ref, wa_ref, wp_ref, own_ref, v_ref, h_ref, d_ref,
                   s_ref, t_ref, hs_ref, ds_ref):
    step = pl.program_id(0)
    row, col = lax.axis_index("row"), lax.axis_index("col")
    width = f_ref.shape[1]
    outs = wp_ref.shape[1]

    @pl.when(step == 0)
    def _():
        hs_ref[...] = jnp.zeros_like(hs_ref)
        ds_ref[...] = jnp.zeros_like(ds_ref)

    for index, (rate, w_ref) in enumerate(zip(RATES, (wc_ref, wb_ref, wa_ref))):
        tall = n + 2 * rate

        for tap in range(3):
            @pl.when(step == 3 * index + tap)
            def _(rate=rate, w_ref=w_ref, tap=tap, tall=tall):
                top = (2 - tap) * rate * n
                if tap == 0:
                    s_ref[:, : tall * n, :] = jnp.zeros((3, tall * n, outs), F32)
                for across in range(3):
                    s_ref[across, top : top + n * n, :] += jnp.dot(
                        f_ref[...], w_ref[0, across], preferred_element_type=F32
                    )

        @pl.when(step == 3 * index + 2)
        def _(rate=rate, tall=tall, index=index):
            t_ref[...] = jnp.zeros_like(t_ref)
            t_ref[:tall, n : 2 * n, :] = s_ref[1, : tall * n, :].reshape(tall, n, outs)
            t_ref[:tall, n + rate : 2 * n + rate, :] += s_ref[0, : tall * n, :].reshape(tall, n, outs)
            t_ref[:tall, n - rate : 2 * n - rate, :] += s_ref[2, : tall * n, :].reshape(tall, n, outs)
            own_ref[3 - index] = t_ref[rate : rate + n, n : 2 * n, :].reshape(n * n, outs)
            vtop = (1 - row) * (n + rate)
            at = SPAN[rate]
            drow, dcol = DIAG[rate]
            v_ref[at : at + rate] = t_ref[pl.ds(vtop, rate), n : 2 * n, :].astype(BF16)
            for side, left in ((0, 2 * n), (1, n - rate)):
                @pl.when(col == side)
                def _(left=left):
                    hs_ref[:, at : at + rate, :] = t_ref[rate : rate + n, left : left + rate, :]
                    ds_ref[drow : drow + rate, dcol : dcol + rate, :] = t_ref[
                        pl.ds(vtop, rate), left : left + rate, :
                    ]

    @pl.when(step == 9)
    def _():
        own_ref[0] = jnp.dot(f_ref[...], wp_ref[...], preferred_element_type=F32)
        h_ref[...] = hs_ref[...].astype(BF16)
        d_ref[...] = ds_ref[...].astype(BF16)


def forward(n, f, wc, wb, wa, wp):
    pix, chans = f.shape
    outs = wp.shape[1]
    whole = lambda shape: pl.BlockSpec(shape, lambda t: (0,) * len(shape))
    taps = lambda first: pl.BlockSpec(
        (1, 3, chans, outs), lambda t: (jnp.clip(t - first, 0, 2), 0, 0, 0)
    )
    shapes = [((4, pix, outs), F32), ((36, n, outs), BF16), ((n, 40, outs), BF16), ((30, n, outs), BF16)]
    return pl.pallas_call(
        functools.partial(forward_kernel, n),
        grid=(10,),
        out_shape=[jax.ShapeDtypeStruct(s, d) for s, d in shapes],
        in_specs=[whole((pix, chans)), taps(0), taps(3), taps(6), whole((chans, outs))],
        out_specs=[whole(s) for s, _ in shapes],
        scratch_shapes=[
            VMEM((3, (n + 36) * n, outs), F32),
            VMEM((n + 36, 3 * n, outs), F32),
            VMEM((n, 40, outs), F32),
            VMEM((30, n, outs), F32),
        ],
        compiler_params=pltpu.CompilerParams(vmem_limit_bytes=LIMIT),
        cost_estimate=pl.CostEstimate(flops=28 * 2 * pix * chans * outs, bytes_accessed=17_000_000, transcendentals=0),
    )(f, wc, wb, wa, wp)


def middle_kernel(n, own_ref, v_ref, h_ref, d_ref, cot_ref, wp_ref, joined_ref, g_ref, d0_ref, d3_ref, v3_ref,
                  acc_ref, hs_ref, ds_ref):
    row, col = lax.axis_index("row"), lax.axis_index("col")
    outs = cot_ref.shape[1]
    pix = n * n
    hs_ref[...] = h_ref[...].astype(F32)
    ds_ref[...] = d_ref[...].astype(F32)
    for index, rate in enumerate(RATES):
        k = 3 - index
        at = SPAN[rate]
        drow, dcol = DIAG[rate]
        vtop = (1 - row) * (n - rate)
        acc_ref[k] = own_ref[k].reshape(n, n, outs)
        acc_ref[k, pl.ds(vtop, rate)] += v_ref[at : at + rate].astype(F32)
        for side, left in ((0, n - rate), (1, 0)):
            @pl.when(col == side)
            def _(left=left):
                acc_ref[k, :, left : left + rate, :] += hs_ref[:, at : at + rate, :]
                acc_ref[k, pl.ds(vtop, rate), left : left + rate, :] += ds_ref[
                    drow : drow + rate, dcol : dcol + rate, :
                ]
    acc_ref[0] = own_ref[0].reshape(n, n, outs)
    for k in range(4):
        pre = acc_ref[k].reshape(pix, outs)
        joined_ref[:, k * outs : (k + 1) * outs] = (pre * jax.nn.sigmoid(pre)).astype(BF16)
    proj_pre = jnp.dot(joined_ref[...], wp_ref[...], preferred_element_type=F32)
    g_ref[...] = (cot_ref[...].astype(F32) * silu_slope(proj_pre)).astype(BF16)
    for k, out_ref in ((0, d0_ref), (3, d3_ref)):
        d_joined = lax.dot_general(
            g_ref[...], wp_ref[k * outs : (k + 1) * outs, :], (((1,), (1,)), ((), ())),
            preferred_element_type=F32,
        )
        out_ref[...] = (d_joined * silu_slope(acc_ref[k].reshape(pix, outs))).astype(BF16)
    v3_ref[...] = d3_ref[pl.ds(pl.multiple_of((1 - row) * ((n - REACH) * n), 16), REACH * n), :]


def middle(n, own, v, h, d, cot, wp):
    pix, outs = cot.shape
    chans = wp.shape[0]
    shapes = [(pix, chans), (pix, outs), (pix, outs), (pix, outs), (REACH * n, outs)]
    return pl.pallas_call(
        functools.partial(middle_kernel, n),
        out_shape=[jax.ShapeDtypeStruct(s, BF16) for s in shapes],
        in_specs=[pl.BlockSpec(memory_space=VMEM)] * 6,
        out_specs=[pl.BlockSpec(memory_space=VMEM)] * 5,
        scratch_shapes=[VMEM((4, n, n, outs), F32), VMEM(h.shape, F32), VMEM(d.shape, F32)],
        compiler_params=pltpu.CompilerParams(vmem_limit_bytes=LIMIT),
    )(own, v, h, d, cot, wp)


def grads_kernel(n, cap, bs_ref, f_ref, joined_ref, g_ref, d0_ref, d3_ref, v3_ref, h3_ref, c3_ref, keep_ref,
                 give_ref, p_ref, pb_ref, ft_ref):
    row, col = lax.axis_index("row"), lax.axis_index("col")
    core = lax.rem(lax.axis_index("dp"), 2)
    pix, outs = g_ref.shape
    chans = f_ref.shape[1]
    per = chans // SROWS
    part = SROWS // 4
    keep_ref[...] = jnp.zeros_like(keep_ref)
    give_ref[...] = jnp.zeros_like(give_ref)

    def place(piece, value):
        for s in range(per):
            slot = bs_ref[piece * per + s]
            owner = slot // cap
            for out_ref, side in ((keep_ref, core), (give_ref, 1 - core)):
                @pl.when(lax.rem(owner, 2) == side)
                def _(out_ref=out_ref):
                    for q in range(4):
                        at = s * SROWS + q * part
                        out_ref[owner // 2, q, slot % cap] = value[at : at + part, :].astype(out_ref.dtype)

    ft_ref[...] = joined_ref[...].T
    place(0, jnp.dot(ft_ref[...], g_ref[...], preferred_element_type=F32))
    ft_ref[...] = f_ref[...].T
    place(1, jnp.dot(ft_ref[...], d0_ref[...], preferred_element_type=F32))

    p_ref[...] = jnp.zeros_like(p_ref)
    p_ref[REACH : REACH + n, n : 2 * n, :] = d3_ref[...].astype(F32).reshape(n, n, outs)
    rtop = (1 - row) * (REACH + n)
    cleft = pl.multiple_of((1 - col) * 2 * n, 8)
    p_ref[pl.ds(rtop, REACH), n : 2 * n, :] = v3_ref[...].astype(F32).reshape(REACH, n, outs)
    p_ref[REACH : REACH + n, pl.ds(cleft, n), :] = h3_ref[...].astype(F32).reshape(n, n, outs)
    p_ref[pl.ds(rtop, REACH), pl.ds(cleft, n), :] = c3_ref[...].astype(F32).reshape(REACH, n, outs)
    tall = n + 2 * REACH
    for across in range(3):
        left = n - (across - 1) * REACH
        pb_ref[across] = p_ref[:, left : left + n, :].reshape(tall * n, outs).astype(BF16)

    def tap(t, carry):
        above, across = t // 3, t % 3
        start = pl.multiple_of((2 - above) * (REACH * n), 16)
        place(2 + t, jnp.dot(ft_ref[...], pb_ref[across, pl.ds(start, pix), :], preferred_element_type=F32))
        return carry

    lax.fori_loop(0, 9, tap, 0)


def grads(n, cap, pairs, bs, f, joined, g, d0, d3, v3, h3, c3):
    pix, chans = f.shape
    outs = g.shape[1]
    return pl.pallas_call(
        functools.partial(grads_kernel, n, cap),
        out_shape=[jax.ShapeDtypeStruct((pairs, 4, cap, SROWS // 4, outs), d) for d in (F32, BF16)],
        in_specs=[pl.BlockSpec(memory_space=pltpu.SMEM)] + [pl.BlockSpec(memory_space=VMEM)] * 8,
        out_specs=[pl.BlockSpec(memory_space=VMEM)] * 2,
        scratch_shapes=[
            VMEM((n + 2 * REACH, 3 * n, outs), F32),
            VMEM((3, (n + 2 * REACH) * n, outs), BF16),
            VMEM((chans, pix), BF16),
        ],
        compiler_params=pltpu.CompilerParams(vmem_limit_bytes=LIMIT),
    )(bs, f, joined, g, d0, d3, v3, h3, c3)


def reduce_kernel(pairs, half, keep_ref, give_ref, out_ref, r_ref, ax_ref, ay_ref, x1_ref, y1_ref, my_ref, mx_ref,
                  y2_ref, x2_ref, fin_ref, z_ref, send, recv):
    row, col, dp = lax.axis_index("row"), lax.axis_index("col"), lax.axis_index("dp")
    core, mine = lax.rem(dp, 2), dp // 2
    depth = keep_ref.shape[2]
    other = {"dp": mine * 2 + 1 - core}
    beside_x = {"row": 1 - row}
    beside_y = {"col": 1 - col}
    zs = [lax.rem(mine + j, pairs) for j in range(pairs)]
    along = [{"dp": zs[j] * 2 + core} for j in range(pairs)]

    barrier = pltpu.get_barrier_semaphore()
    partners = [other, beside_x, beside_y] + along[1:]
    for partner in partners:
        pl.semaphore_signal(barrier, inc=1, device_id=partner, device_id_type=MESH)
    pl.semaphore_wait(barrier, len(partners))

    def copy(kind, j, src, dst, where):
        return pltpu.make_async_remote_copy(
            src_ref=src, dst_ref=dst, send_sem=send.at[kind, j], recv_sem=recv.at[kind, j],
            device_id=where, device_id_type=MESH,
        )

    order = list(range(1, pairs)) + [0]
    low, high = pl.ds(0, half), pl.ds(half, depth - half)
    cores = {j: copy(0, j, give_ref.at[zs[j]], r_ref.at[j], other) for j in order}
    for j in order:
        cores[j].start()
    x1, y1, x2, y2, along_z = {}, {}, {}, {}, {}

    def pair(j, r, c, rows):
        return keep_ref[zs[j], r * 2 + c, rows, :] + r_ref[j, r * 2 + c, rows, :].astype(F32)

    def first(j):
        cores[j].wait_recv()
        for k in range(2):
            ax_ref[j, k] = pair(j, 1 - row, k, low).astype(BF16)
            ay_ref[j, k] = pair(j, k, 1 - col, high).astype(BF16)
        x1[j] = copy(1, j, ax_ref.at[j], x1_ref.at[j], beside_x)
        y1[j] = copy(2, j, ay_ref.at[j], y1_ref.at[j], beside_y)
        x1[j].start()
        y1[j].start()

    def second(j):
        x1[j].wait_recv()
        my_ref[j] = (pair(j, row, 1 - col, low) + x1_ref[j, 1 - col].astype(F32)).astype(BF16)
        y2[j] = copy(3, j, my_ref.at[j], y2_ref.at[j], beside_y)
        y2[j].start()
        y1[j].wait_recv()
        mx_ref[j] = (pair(j, 1 - row, col, high) + y1_ref[j, 1 - row].astype(F32)).astype(BF16)
        x2[j] = copy(4, j, mx_ref.at[j], x2_ref.at[j], beside_x)
        x2[j].start()

    def third(j):
        y2[j].wait_recv()
        x2[j].wait_recv()
        lower = pair(j, row, col, low) + x1_ref[j, col].astype(F32) + y2_ref[j].astype(F32)
        upper = pair(j, row, col, high) + y1_ref[j, row].astype(F32) + x2_ref[j].astype(F32)
        if j == 0:
            out_ref[low, :] = lower
            out_ref[high, :] = upper
        else:
            fin_ref[j, low, :] = lower.astype(BF16)
            fin_ref[j, high, :] = upper.astype(BF16)
            along_z[j] = copy(5, j, fin_ref.at[j], z_ref.at[j], along[j])
            along_z[j].start()

    for at in range(pairs + 2):
        if at < pairs:
            first(order[at])
        if 1 <= at <= pairs:
            second(order[at - 1])
        if at >= 2:
            third(order[at - 2])
    for j in order[:-1]:
        along_z[j].wait_recv()
        out_ref[...] += z_ref[j].astype(F32)
    for j in order:
        for group in (cores, x1, y1, x2, y2):
            group[j].wait_send()
        if j:
            along_z[j].wait_send()


def reduce_scatter(keep, give):
    pairs, quarters, depth, outs = keep.shape
    half = (depth // 16 + 1) // 2 * 16
    rest = depth - half
    buf = lambda *shape: VMEM(shape + (outs,), BF16)
    return pl.pallas_call(
        functools.partial(reduce_kernel, pairs, half),
        out_shape=jax.ShapeDtypeStruct((depth, outs), F32),
        in_specs=[pl.BlockSpec(memory_space=VMEM)] * 2,
        out_specs=pl.BlockSpec(memory_space=VMEM),
        scratch_shapes=[
            buf(pairs, quarters, depth),
            buf(pairs, 2, half),
            buf(pairs, 2, rest),
            buf(pairs, 2, half),
            buf(pairs, 2, rest),
            buf(pairs, half),
            buf(pairs, rest),
            buf(pairs, half),
            buf(pairs, rest),
            buf(pairs, depth),
            buf(pairs, depth),
            pltpu.SemaphoreType.DMA((6, pairs)),
            pltpu.SemaphoreType.DMA((6, pairs)),
        ],
        compiler_params=pltpu.CompilerParams(
            collective_id=0, has_side_effects=True, vmem_limit_bytes=LIMIT
        ),
    )(keep, give)


def shards(features, cotangent, w_point, w_rate_a, w_rate_b, w_rate_c, w_proj, bucket_slot):
    n = features.shape[1]
    chans = features.shape[3]
    outs = w_point.shape[1]
    pix = n * n
    f = features.reshape(pix, chans)
    cot = cotangent.reshape(pix, outs)
    swap = [(0, 1), (1, 0)]
    cross = [(i, 3 - i) for i in range(4)]
    replicas = lax.axis_size("dp")
    nslice = bucket_slot.shape[0]
    cap = nslice // replicas + 1
    own, v, h, d = forward(n, f, w_rate_c, w_rate_b, w_rate_a, w_point)
    d = lax.ppermute(d, ("row", "col"), cross)
    v = lax.ppermute(v, "row", swap)
    h = lax.ppermute(h, "col", swap)
    joined, g, d0, d3, v3 = middle(n, own, v, h, d, cot, w_proj)
    c3 = lax.ppermute(v3, ("row", "col"), cross)
    v3 = lax.ppermute(v3, "row", swap)
    h3 = lax.ppermute(d3, "col", swap)
    keep, give = grads(n, cap, replicas // 2, bucket_slot, f, joined, g, d0, d3, v3, h3, c3)
    shape = (replicas // 2, 4, cap * (SROWS // 4), outs)
    total = reduce_scatter(keep.reshape(shape), give.reshape(shape))
    return total.reshape(cap, SROWS // 4 * outs)


def solution(mesh):
    placed = (
        P("dp", "row", "col", None),
        P("dp", "row", "col", None),
        P(),
        P(),
        P(),
        P(),
        P(),
        P(),
    )
    return jax.shard_map(
        shards, mesh=mesh, in_specs=placed, out_specs=P("dp", ("row", "col")), check_vma=False
    )
```

time: 372 us -> 124 us (0.33); the launches traced: 365 us -> 123 us
  waiting for transfers between devices: 166 us -> 26.6 us
  Pallas kernels: 0 us -> 87.1 us
  matrix products: 72.5 us -> 0 us
  local copies, waits for them, and re-layouts: 55.2 us -> 3.57 us
  blocking collectives: 34.9 us -> 0 us
  between operations: 15.3 us -> 0.03 us
  starting transfers between devices: 14.3 us -> 5.95 us
  other arithmetic: 6.11 us -> 0 us
    reduce_scatter x1 -> x0, waiting for transfers between devices: 118 us -> none  [shards(): lax.psum_scatter(buffer, ('row', 'col'), scatter_dimension=1, tiled=True)]
    pallas_call x0 -> x4, Pallas kernels: none -> 87.1 us  [the longest x1 43.7 us: reduce_scatter(): pl.pallas_call(functools.partial(reduce_kernel, pairs, half), out_shape=j...]
    dot_general x41 -> x0, matrix products: 72.5 us -> none  [the longest x27 51.7 us: shards(): jnp.dot(window(rate, above - 1, across - 1), kernel[above, across], prefe...]
    unnamed x1 -> x0, blocking collectives: 34.9 us -> none
    slice x5 -> x0, local copies, waits for them, and re-layouts: 20.7 us -> none  [the longest x1 14.8 us: window(): padded[top:top + rows_dev, left:left + cols_dev].reshape(pixels, chans)]
    ppermute x4 -> x6, waiting for transfers between devices: 46.9 us -> 26.6 us  [the longest x1 17.7 us: shards(): d = lax.ppermute(d, ('row', 'col'), cross)]
    scatter x1 -> x0, local copies, waits for them, and re-layouts: 15.5 us -> none  [shards(): jnp.zeros((slot_count, slices.shape[1]), jnp.float32).at[bucket_slot]]
    reshape x1, local copies, waits for them, and re-layouts: 13.5 us -> 1.81 us  [shards(): return total.reshape(cap, SROWS // 4 * outs)]
  transfers between devices with their start and end apart: 6 -> 6, of which waited for: 6 -> 4; matrix products, arithmetic and copies ran while one was open for 7% -> 0% of each run, Pallas kernels for 0% -> 0%
where the time goes in v1:
time: 124 us; the launch traced here: 123 us
  Pallas kernels  87.1 us (70%)
  waiting for transfers between devices  26.6 us (21%)
  starting transfers between devices  5.95 us (5%)
  local copies, waits for them, and re-layouts  3.57 us (3%)
    pallas_call x1, Pallas kernels, reduce_scatter(): pl.pallas_call(functools.partial(reduce_kernel, pairs, half), out_shape=j...  43.7 us
    pallas_call x1, Pallas kernels, grads(): pl.pallas_call(functools.partial(grads_kernel, n, cap), out_shape=[jax.Sh...  19.9 us
    pallas_call x1, Pallas kernels, forward(): pl.pallas_call(functools.partial(forward_kernel, n), grid=(10,), out_shap...  18.4 us
    ppermute x1, waiting for transfers between devices, shards(): d = lax.ppermute(d, ('row', 'col'), cross)  17.7 us
    pallas_call x1, Pallas kernels, middle(): pl.pallas_call(functools.partial(middle_kernel, n), out_shape=[jax.ShapeD...  5.15 us
    ppermute x1, waiting for transfers between devices, shards(): c3 = lax.ppermute(v3, ('row', 'col'), cross)  4.42 us
    ppermute x1, waiting for transfers between devices, shards(): v3 = lax.ppermute(v3, 'row', swap)  4.25 us
  transfers between devices with their start and end apart: 6, of which 4 were waited for; matrix products, arithmetic and copies ran while one was open for 0% of the time, Pallas kernels for 0%

profile of v1, /device:TPU:1, one launch (start us, length us, event | category | flops | bytes accessed | tf_op | source)
XLA Modules:
  0.0 123.3 jit_solution(11178452404046575733)
XLA Ops:
  0.0 18.4 %shard_map.82 = (f32[4,576,256]{2,1,0:T(8,128)}, bf16[36,24,256]{2,1,0:T(8,128)(2,1)}, bf16[24,40,256]{2,1,0:T(8,128)(2,1)}, bf16[30,24,256]{2,1,0:T(8,128)(2,1)}) custom-call(bf16[576,1024]{1,0:T(8,128)(2,1)} %bitcast.6, bf16[3,3,1024,256]{3,2,1,0:T(8,128)(2,1)} %wc_ref.1, bf16[3,3,1024,256]{3,2,1,0:T(8,128)(2,1)} %wb_ref.1, ...), custom_call_target="tpu_custom_call" | custom-call | flops 8455716864 | bytes 17000000 | tf_op jit(solution)/shard_map/pallas_call | solution.py:87
  18.4 2.1 %collective-permute-start.1 = (bf16[24,40,256]{2,1,0:T(8,128)(2,1)}, bf16[24,40,256]{2,1,0:T(8,128)(2,1)S(1)}, u32[]{:S(2)}, u32[]{:S(2)}) collective-permute-start(bf16[24,40,256]{2,1,0:T(8,128)(2,1)} %get-tuple-element.18), channel_id=1, source_target_pairs={{0,8},{8,0},{1,9},{9,1},{2,10},{10,2},{3,11},{11,3},{4,12},{12,4},... | collective-permute-start | bytes 1474568 | tf_op jit(solution)/shard_map/ppermute | solution.py:349
  20.5 1.2 collective-permute-start
  21.7 0.0 collective-permute-start.2
  21.7 17.7 %collective-permute-done.2.d_ref = bf16[30,24,256]{2,1,0:T(8,128)(2,1)S(1)} collective-permute-done((bf16[30,24,256]{2,1,0:T(8,128)(2,1)}, bf16[30,24,256]{2,1,0:T(8,128)(2,1)S(1)}, u32[]{:S(2)}, u32[]{:S(2)}) %collective-permute-start.2) | collective-permute-done | bytes 368672 | tf_op jit(solution)/shard_map/ppermute | solution.py:347
  39.4 0.0 copy-start.2
  39.4 0.0 collective-permute-done.v_ref
  39.4 0.0 copy-start.1
  39.4 0.0 collective-permute-done.1.h_ref
  39.4 0.0 copy-start
  39.4 0.7 copy-done.2
  40.1 0.1 copy-done.1
  40.3 0.2 copy-done
  40.5 5.1 %shard_map.83 = (bf16[576,1024]{1,0:T(8,128)(2,1)}, bf16[576,256]{1,0:T(8,128)(2,1)}, bf16[576,256]{1,0:T(8,128)(2,1)}, bf16[576,256]{1,0:T(8,128)(2,1)}, bf16[432,256]{1,0:T(8,128)(2,1)}) custom-call(f32[4,576,256]{2,1,0:T(8,128)} %get-tuple-element.16.own_ref, bf16[36,24,256]{2,1,0:T(8,128)(2,1)} %copy-done.1, bf16[24,40,256]{2,1,0:T(8,128)(2,1)} %copy-done, ...), custom_call_target="tpu_custom_call" | custom-call | tf_op jit(solution)/shard_map/pallas_call | solution.py:144
  45.6 1.1 collective-permute-start.4
  46.7 1.2 collective-permute-start.5
  47.9 0.4 collective-permute-start.3
  48.3 4.4 %collective-permute-done.5.c3_ref = bf16[432,256]{1,0:T(8,128)(2,1)S(1)} collective-permute-done((bf16[432,256]{1,0:T(8,128)(2,1)}, bf16[432,256]{1,0:T(8,128)(2,1)S(1)}, u32[]{:S(2)}, u32[]{:S(2)}) %collective-permute-start.5) | collective-permute-done | bytes 221216 | tf_op jit(solution)/shard_map/ppermute | solution.py:351
  52.7 0.0 copy-start.4
  52.7 4.2 %collective-permute-done.3.v3_ref = bf16[432,256]{1,0:T(8,128)(2,1)S(1)} collective-permute-done((bf16[432,256]{1,0:T(8,128)(2,1)}, bf16[432,256]{1,0:T(8,128)(2,1)S(1)}, u32[]{:S(2)}, u32[]{:S(2)}) %collective-permute-start.3) | collective-permute-done | bytes 221216 | tf_op jit(solution)/shard_map/ppermute | solution.py:352
  56.9 0.0 copy-start.5
  56.9 0.2 collective-permute-done.4.h3_ref
  57.1 0.0 copy-start.3
  57.1 0.0 copy-done.4
  57.1 0.5 copy-done.5
  57.6 0.3 copy-done.3
  57.9 19.9 %shard_map.84 = (f32[4,4,23,16,256]{4,3,2,1,0:T(8,128)}, bf16[4,4,23,16,256]{4,3,2,1,0:T(8,128)(2,1)}) custom-call(s32[176]{0:T(256)} %bs_ref.1, bf16[576,1024]{1,0:T(8,128)(2,1)} %bitcast.7, bf16[576,1024]{1,0:T(8,128)(2,1)} %get-tuple-element.20.joined_ref, bf16[576,256]{1,0:T(8,128)(2,1)} %get-tuple-element.21.g_ref, ...), custom_call_target="tpu_custom_call" | custom-call | tf_op jit(solution)/shard_map/pallas_call | solution.py:205
  77.8 43.7 %shard_map.85 = f32[368,256]{1,0:T(8,128)} custom-call(f32[4,4,368,256]{3,2,1,0:T(8,128)} %bitcast.4, bf16[4,4,368,256]{3,2,1,0:T(8,128)(2,1)} %bitcast.5), custom_call_target="tpu_custom_call" | custom-call | tf_op jit(solution)/shard_map/pallas_call | solution.py:308
  121.5 1.8 %reshape.19 = f32[23,4096]{1,0:T(8,128)} reshape(f32[368,256]{1,0:T(8,128)} %shard_map.85) | data formatting | bytes 753664 | tf_op jit(solution)/shard_map/reshape | solution.py:357
Async XLA Ops:
  18.4 21.0 %collective-permute-start.1 = (bf16[24,40,256]{2,1,0:T(8,128)(2,1)}, bf16[24,40,256]{2,1,0:T(8,128)(2,1)S(1)}, u32[]{:S(2)}, u32[]{:S(2)}) collective-permute-start(bf16[24,40,256]{2,1,0:T(8,128)(2,1)} %get-tuple-element.18), channel_id=1, source_target_pairs={{0,8},{8,0},{1,9},{9,1},{2,10},{10,2},{3,11},{11,3},{4,12},{12,4},... | collective-permute-start | bytes 1474568 | tf_op jit(solution)/shard_map/ppermute | solution.py:349
  20.5 18.9 %collective-permute-start = (bf16[36,24,256]{2,1,0:T(8,128)(2,1)}, bf16[36,24,256]{2,1,0:T(8,128)(2,1)S(1)}, u32[]{:S(2)}, u32[]{:S(2)}) collective-permute-start(bf16[36,24,256]{2,1,0:T(8,128)(2,1)} %get-tuple-element.17), channel_id=1, source_target_pairs={{0,16},{16,0},{1,17},{17,1},{2,18},{18,2},{3,19},{19,3},{4,20},{20... | collective-permute-start | bytes 1327112 | tf_op jit(solution)/shard_map/ppermute | solution.py:348
  21.7 17.7 %collective-permute-start.2 = (bf16[30,24,256]{2,1,0:T(8,128)(2,1)}, bf16[30,24,256]{2,1,0:T(8,128)(2,1)S(1)}, u32[]{:S(2)}, u32[]{:S(2)}) collective-permute-start(bf16[30,24,256]{2,1,0:T(8,128)(2,1)} %get-tuple-element.19), channel_id=1, source_target_pairs={{0,24},{8,16},{16,8},{24,0},{1,25},{9,17},{17,9},{25,1},{2,26},{10... | collective-permute-start | bytes 1105928 | tf_op jit(solution)/shard_map/ppermute | solution.py:347
  39.4 0.7 copy-start.2
  39.4 0.9 copy-start.1
  39.4 1.1 copy-start
  45.6 11.5 %collective-permute-start.4 = (bf16[576,256]{1,0:T(8,128)(2,1)}, bf16[576,256]{1,0:T(8,128)(2,1)S(1)}, u32[]{:S(2)}, u32[]{:S(2)}) collective-permute-start(bf16[576,256]{1,0:T(8,128)(2,1)} %get-tuple-element.23.d3_ref), channel_id=1, source_target_pairs={{0,8},{8,0},{1,9},{9,1},{2,10},{10,2},{3,11},{11,3},{4,12},{12,4},... | collective-permute-start | bytes 884744 | tf_op jit(solution)/shard_map/ppermute | solution.py:353
  46.7 6.0 %collective-permute-start.5 = (bf16[432,256]{1,0:T(8,128)(2,1)}, bf16[432,256]{1,0:T(8,128)(2,1)S(1)}, u32[]{:S(2)}, u32[]{:S(2)}) collective-permute-start(bf16[432,256]{1,0:T(8,128)(2,1)} %get-tuple-element.24), channel_id=1, source_target_pairs={{0,24},{8,16},{16,8},{24,0},{1,25},{9,17},{17,9},{25,1},{2,26},{10... | collective-permute-start | bytes 663560 | tf_op jit(solution)/shard_map/ppermute | solution.py:351
  47.9 9.1 %collective-permute-start.3 = (bf16[432,256]{1,0:T(8,128)(2,1)}, bf16[432,256]{1,0:T(8,128)(2,1)S(1)}, u32[]{:S(2)}, u32[]{:S(2)}) collective-permute-start(bf16[432,256]{1,0:T(8,128)(2,1)} %get-tuple-element.24), channel_id=1, source_target_pairs={{0,16},{16,0},{1,17},{17,1},{2,18},{18,2},{3,19},{19,3},{4,20},{20... | collective-permute-start | bytes 663560 | tf_op jit(solution)/shard_map/ppermute | solution.py:352
  52.7 4.5 %copy-start.4 = (bf16[432,256]{1,0:T(8,128)(2,1)}, bf16[432,256]{1,0:T(8,128)(2,1)S(1)}, u32[]{:S(2)}) copy-start(bf16[432,256]{1,0:T(8,128)(2,1)S(1)} %collective-permute-done.5.c3_ref) | copy-start | bytes 663556
  56.9 0.7 copy-start.5
  57.1 0.7 copy-start.3

commit v2 on v1

v2 whole, which is shorter than its diff:
```python
import functools

import jax
import jax.numpy as jnp
from jax import lax
from jax.experimental import pallas as pl
from jax.experimental.pallas import tpu as pltpu
from jax.sharding import PartitionSpec as P

RATES = (18, 12, 6)
REACH = 18
SROWS = 64
MESH = pl.DeviceIdType.MESH
VMEM = pltpu.VMEM
BF16 = jnp.bfloat16
F32 = jnp.float32
LIMIT = 56 * 1024 * 1024


def silu_slope(value):
    sig = jax.nn.sigmoid(value)
    return sig * (1.0 + value * (1.0 - sig))


def padded_rows(count):
    return -(-count // 16) * 16


def edge_sizes(n):
    v, h, d = {}, {}, {}
    tops = [0, 0, 0]
    for rate in RATES:
        for k, (table, size) in enumerate(((v, rate * n), (h, n * rate), (d, rate * rate))):
            table[rate] = pl.ds(tops[k], padded_rows(size))
            tops[k] += padded_rows(size)
    return (v, h, d), tops


def forward_kernel(n, f_ref, wc_ref, wb_ref, wa_ref, wp_ref, cot_ref, wq_ref, g01_ref, ft_ref, pb_ref,
                   s_ref, t_ref, acc_ref, strip, vs_ref, hs_ref, ds_ref, vr_ref, hr_ref, dr_ref,
                   joined_ref, jt_ref, g_ref, d0_ref, d3_ref, v3_ref, h3_ref, c3_ref, h3s_ref, c3s_ref,
                   send, recv):
    step = pl.program_id(0)
    row, col = lax.axis_index("row"), lax.axis_index("col")
    outs = wp_ref.shape[1]
    pix = n * n
    spans, unused = edge_sizes(n)

    def cut(src, top, rows, rate, lefts):
        for side, left in enumerate(lefts):
            @pl.when(col == side)
            def _(left=left):
                for i in range(rows):
                    strip[i * rate : (i + 1) * rate, :] = src[top + i, left : left + rate, :]
        return strip[: padded_rows(rows * rate), :].astype(BF16)

    def paste(dst, top, rows, rate, lefts, value):
        strip[: value.shape[0], :] = value.astype(F32)
        for side, left in enumerate(lefts):
            @pl.when(col == side)
            def _(left=left):
                for i in range(rows):
                    dst[top + i, left : left + rate, :] += strip[i * rate : (i + 1) * rate, :]

    beside = ({"row": 1 - row}, {"col": 1 - col}, {"row": 1 - row, "col": 1 - col})

    def copy(kind, which, src, dst):
        return pltpu.make_async_remote_copy(
            src_ref=src, dst_ref=dst, send_sem=send.at[kind, which], recv_sem=recv.at[kind, which],
            device_id=beside[kind], device_id_type=MESH,
        )

    def edges(index):
        rate = RATES[index]
        pairs = ((vs_ref, vr_ref), (hs_ref, hr_ref), (ds_ref, dr_ref))
        return [
            copy(k, index, src.at[spans[k][rate]], dst.at[spans[k][rate]])
            for k, (src, dst) in enumerate(pairs)
        ]

    @pl.when(step == 0)
    def _():
        barrier = pltpu.get_barrier_semaphore()
        for where in beside:
            pl.semaphore_signal(barrier, inc=1, device_id=where, device_id_type=MESH)
        pl.semaphore_wait(barrier, 3)
        strip[...] = jnp.zeros_like(strip)

    for index, (rate, w_ref) in enumerate(zip(RATES, (wc_ref, wb_ref, wa_ref))):
        tall = n + 2 * rate

        for tap in range(3):
            @pl.when(step == 3 * index + tap)
            def _(rate=rate, w_ref=w_ref, tap=tap, tall=tall):
                top = (2 - tap) * rate * n
                if tap == 0:
                    s_ref[:, : tall * n, :] = jnp.zeros((3, tall * n, outs), F32)
                for across in range(3):
                    s_ref[across, top : top + pix, :] += jnp.dot(
                        f_ref[...], w_ref[0, across], preferred_element_type=F32
                    )

        @pl.when(step == 3 * index + 2)
        def _(rate=rate, tall=tall, index=index):
            t_ref[...] = jnp.zeros_like(t_ref)
            t_ref[:tall, n : 2 * n, :] = s_ref[1, : tall * n, :].reshape(tall, n, outs)
            t_ref[:tall, n + rate : 2 * n + rate, :] += s_ref[0, : tall * n, :].reshape(tall, n, outs)
            t_ref[:tall, n - rate : 2 * n - rate, :] += s_ref[2, : tall * n, :].reshape(tall, n, outs)
            vtop = (1 - row) * (n + rate)
            vs_ref[spans[0][rate], :] = (
                t_ref[pl.ds(vtop, rate), n : 2 * n, :].reshape(rate * n, outs).astype(BF16)
            )
            lefts = (2 * n, n - rate)
            hs_ref[spans[1][rate], :] = cut(t_ref, rate, n, rate, lefts)
            ds_ref[spans[2][rate], :] = cut(t_ref, vtop, rate, rate, lefts)
            for edge in edges(index):
                edge.start()
            acc_ref[3 - index] = t_ref[rate : rate + n, n : 2 * n, :]

    @pl.when(step == 9)
    def _():
        acc_ref[0] = jnp.dot(f_ref[...], wp_ref[...], preferred_element_type=F32).reshape(n, n, outs)
        ft_ref[...] = f_ref[...].T
        for index, rate in enumerate(RATES):
            k = 3 - index
            vtop = (1 - row) * (n - rate)
            v_edge, h_edge, d_edge = edges(index)
            v_edge.wait_recv()
            acc_ref[k, pl.ds(vtop, rate)] += vr_ref[spans[0][rate], :].astype(F32).reshape(rate, n, outs)

            lefts = (n - rate, 0)
            h_edge.wait_recv()
            paste(acc_ref.at[k], 0, n, rate, lefts, hr_ref[spans[1][rate], :])
            d_edge.wait_recv()
            paste(acc_ref.at[k], vtop, rate, rate, lefts, dr_ref[spans[2][rate], :])
        for k in range(4):
            pre = acc_ref[k].reshape(pix, outs)
            joined_ref[:, k * outs : (k + 1) * outs] = (pre * jax.nn.sigmoid(pre)).astype(BF16)
        proj_pre = jnp.dot(joined_ref[...], wq_ref[...], preferred_element_type=F32)
        g_ref[...] = (cot_ref[...].astype(F32) * silu_slope(proj_pre)).astype(BF16)
        for k, out_ref in ((3, d3_ref), (0, d0_ref)):
            d_joined = lax.dot_general(
                g_ref[...], wq_ref[k * outs : (k + 1) * outs, :], (((1,), (1,)), ((), ())),
                preferred_element_type=F32,
            )
            out_ref[...] = (d_joined * silu_slope(acc_ref[k].reshape(pix, outs))).astype(BF16)
            if k == 3:
                part = pl.ds(pl.multiple_of((1 - row) * ((n - REACH) * n), 16), REACH * n)
                v3 = copy(0, 3, d3_ref.at[part], v3_ref)
                v3.start()
                acc_ref[3] = d3_ref[...].astype(F32).reshape(n, n, outs)
                lefts = (n - REACH, 0)
                h3s_ref[...] = cut(acc_ref.at[3], 0, n, REACH, lefts)
                h3 = copy(1, 3, h3s_ref, h3_ref)
                h3.start()
                c3s_ref[...] = cut(acc_ref.at[3], (1 - row) * (n - REACH), REACH, REACH, lefts)
                c3 = copy(2, 3, c3s_ref, c3_ref)
                c3.start()
        chans = joined_ref.shape[1]
        jt_ref[...] = joined_ref[...].T
        g01_ref[:chans, :] = jnp.dot(jt_ref[...], g_ref[...], preferred_element_type=F32)
        g01_ref[chans:, :] = jnp.dot(ft_ref[...], d0_ref[...], preferred_element_type=F32)
        t_ref[...] = jnp.zeros_like(t_ref)
        t_ref[REACH : REACH + n, n : 2 * n, :] = d3_ref[...].astype(F32).reshape(n, n, outs)
        rtop = (1 - row) * (REACH + n)
        lefts = (2 * n, n - REACH)
        v3.wait_recv()
        t_ref[pl.ds(rtop, REACH), n : 2 * n, :] = v3_ref[...].astype(F32).reshape(REACH, n, outs)
        h3.wait_recv()
        paste(t_ref, REACH, n, REACH, lefts, h3_ref[...])
        c3.wait_recv()
        paste(t_ref, rtop, REACH, REACH, lefts, c3_ref[...])
        tall = n + 2 * REACH
        for across in range(3):
            left = n - (across - 1) * REACH
            pb_ref[:, across * outs : (across + 1) * outs] = t_ref[:, left : left + n, :].reshape(tall * n, outs).astype(BF16)
        for index in range(3):
            for edge in edges(index):
                edge.wait_send()
        for edge in (c3, h3, v3):
            edge.wait_send()


def forward(n, f, wc, wb, wa, wp, cot, wq):
    pix, chans = f.shape
    outs = wp.shape[1]
    whole = lambda shape: pl.BlockSpec(shape, lambda t: (0,) * len(shape))
    taps = lambda first: pl.BlockSpec(
        (1, 3, chans, outs), lambda t: (jnp.clip(t - first, 0, 2), 0, 0, 0)
    )
    unused, tops = edge_sizes(n)
    corner = padded_rows(REACH * REACH)
    tall = n + 2 * REACH
    shapes = [((2 * chans, outs), F32), ((chans, pix), BF16), ((tall * n, 3 * outs), BF16)]
    return pl.pallas_call(
        functools.partial(forward_kernel, n),
        grid=(10,),
        out_shape=[jax.ShapeDtypeStruct(s, d) for s, d in shapes],
        in_specs=[whole((pix, chans)), taps(0), taps(3), taps(6), whole((chans, outs)), whole((pix, outs)),
                  whole((chans, outs))],
        out_specs=[whole(s) for s, _ in shapes],
        scratch_shapes=[
            VMEM((3, tall * n, outs), F32),
            VMEM((tall, 3 * n, outs), F32),
            VMEM((4, n, n, outs), F32),
            VMEM((REACH * n, outs), F32),
        ]
        + [VMEM((top, outs), BF16) for top in tops] * 2
        + [
            VMEM((pix, chans), BF16),
            VMEM((chans, pix), BF16),
            VMEM((pix, outs), BF16),
            VMEM((pix, outs), BF16),
            VMEM((pix, outs), BF16),
            VMEM((REACH * n, outs), BF16),
            VMEM((REACH * n, outs), BF16),
            VMEM((corner, outs), BF16),
            VMEM((REACH * n, outs), BF16),
            VMEM((corner, outs), BF16),
            pltpu.SemaphoreType.DMA((3, 4)),
            pltpu.SemaphoreType.DMA((3, 4)),
        ],
        compiler_params=pltpu.CompilerParams(
            collective_id=1, has_side_effects=True, vmem_limit_bytes=LIMIT
        ),
    )(f, wc, wb, wa, wp, cot, wq)


def grads_kernel(n, cap, bs_ref, g01_ref, ft_ref, pb_ref, keep_ref, give_ref):
    core = lax.rem(lax.axis_index("dp"), 2)
    chans, pix = ft_ref.shape
    per = chans // SROWS
    part = SROWS // 4
    keep_ref[...] = jnp.zeros_like(keep_ref)
    give_ref[...] = jnp.zeros_like(give_ref)

    def place(piece, value):
        for s in range(per):
            slot = bs_ref[piece * per + s]
            owner = slot // cap
            for out_ref, side in ((keep_ref, core), (give_ref, 1 - core)):
                @pl.when(lax.rem(owner, 2) == side)
                def _(out_ref=out_ref):
                    for q in range(4):
                        at = s * SROWS + q * part
                        out_ref[owner // 2, q, slot % cap] = value[at : at + part, :].astype(out_ref.dtype)

    for piece in range(2):
        place(piece, g01_ref[piece * chans : (piece + 1) * chans, :])

    def line(above, carry):
        start = pl.multiple_of((2 - above) * (REACH * n), 16)
        value = jnp.dot(ft_ref[...], pb_ref[pl.ds(start, pix), :], preferred_element_type=F32)
        outs = value.shape[1] // 3
        for across in range(3):
            place(2 + 3 * above + across, value[:, across * outs : (across + 1) * outs])
        return carry

    lax.fori_loop(0, 3, line, 0)


def grads(n, cap, pairs, bs, g01, ft, pb):
    outs = g01.shape[1]
    return pl.pallas_call(
        functools.partial(grads_kernel, n, cap),
        out_shape=[jax.ShapeDtypeStruct((pairs, 4, cap, SROWS // 4, outs), d) for d in (F32, BF16)],
        in_specs=[pl.BlockSpec(memory_space=pltpu.SMEM)] + [pl.BlockSpec(memory_space=VMEM)] * 3,
        out_specs=[pl.BlockSpec(memory_space=VMEM)] * 2,
        compiler_params=pltpu.CompilerParams(vmem_limit_bytes=LIMIT),
    )(bs, g01, ft, pb)


def reduce_kernel(pairs, half, held_ref, give_ref, out_ref, keep_ref, r_ref, ax_ref, ay_ref, x1_ref, y1_ref, my_ref, mx_ref,
                  y2_ref, x2_ref, fin_ref, z_ref, send, recv, load):
    row, col, dp = lax.axis_index("row"), lax.axis_index("col"), lax.axis_index("dp")
    core, mine = lax.rem(dp, 2), dp // 2
    depth = keep_ref.shape[2]
    other = {"dp": mine * 2 + 1 - core}
    beside_x = {"row": 1 - row}
    beside_y = {"col": 1 - col}
    zs = [lax.rem(mine + j, pairs) for j in range(pairs)]
    along = [{"dp": zs[j] * 2 + core} for j in range(pairs)]

    fetch = pltpu.make_async_copy(held_ref, keep_ref, load)
    fetch.start()
    barrier = pltpu.get_barrier_semaphore()
    partners = [other, beside_x, beside_y] + along[1:]
    for partner in partners:
        pl.semaphore_signal(barrier, inc=1, device_id=partner, device_id_type=MESH)
    pl.semaphore_wait(barrier, len(partners))

    def copy(kind, j, src, dst, where):
        return pltpu.make_async_remote_copy(
            src_ref=src, dst_ref=dst, send_sem=send.at[kind, j], recv_sem=recv.at[kind, j],
            device_id=where, device_id_type=MESH,
        )

    order = list(range(1, pairs)) + [0]
    low, high = pl.ds(0, half), pl.ds(half, depth - half)
    cores = {j: copy(0, j, give_ref.at[zs[j]], r_ref.at[j], other) for j in order}
    for j in order:
        cores[j].start()
    fetch.wait()
    x1, y1, x2, y2, along_z = {}, {}, {}, {}, {}

    def pair(j, r, c, rows):
        return keep_ref[zs[j], r * 2 + c, rows, :] + r_ref[j, r * 2 + c, rows, :].astype(F32)

    def first(j):
        cores[j].wait_recv()
        for k in range(2):
            ax_ref[j, k] = pair(j, 1 - row, k, low).astype(BF16)
            ay_ref[j, k] = pair(j, k, 1 - col, high).astype(BF16)
        x1[j] = copy(1, j, ax_ref.at[j], x1_ref.at[j], beside_x)
        y1[j] = copy(2, j, ay_ref.at[j], y1_ref.at[j], beside_y)
        x1[j].start()
        y1[j].start()

    def second(j):
        x1[j].wait_recv()
        my_ref[j] = (pair(j, row, 1 - col, low) + x1_ref[j, 1 - col].astype(F32)).astype(BF16)
        y2[j] = copy(3, j, my_ref.at[j], y2_ref.at[j], beside_y)
        y2[j].start()
        y1[j].wait_recv()
        mx_ref[j] = (pair(j, 1 - row, col, high) + y1_ref[j, 1 - row].astype(F32)).astype(BF16)
        x2[j] = copy(4, j, mx_ref.at[j], x2_ref.at[j], beside_x)
        x2[j].start()

    def third(j):
        y2[j].wait_recv()
        x2[j].wait_recv()
        lower = pair(j, row, col, low) + x1_ref[j, col].astype(F32) + y2_ref[j].astype(F32)
        upper = pair(j, row, col, high) + y1_ref[j, row].astype(F32) + x2_ref[j].astype(F32)
        if j == 0:
            out_ref[low, :] = lower
            out_ref[high, :] = upper
        else:
            fin_ref[j, low, :] = lower.astype(BF16)
            fin_ref[j, high, :] = upper.astype(BF16)
            along_z[j] = copy(5, j, fin_ref.at[j], z_ref.at[j], along[j])
            along_z[j].start()

    for at in range(pairs + 2):
        if at < pairs:
            first(order[at])
        if 1 <= at <= pairs:
            second(order[at - 1])
        if at >= 2:
            third(order[at - 2])
    for j in order[:-1]:
        along_z[j].wait_recv()
        out_ref[...] += z_ref[j].astype(F32)
    for j in order:
        for group in (cores, x1, y1, x2, y2):
            group[j].wait_send()
        if j:
            along_z[j].wait_send()


def reduce_scatter(keep, give):
    pairs, quarters, depth, outs = keep.shape
    half = (depth // 16 + 1) // 2 * 16
    rest = depth - half
    buf = lambda *shape: VMEM(shape + (outs,), BF16)
    return pl.pallas_call(
        functools.partial(reduce_kernel, pairs, half),
        out_shape=jax.ShapeDtypeStruct((depth, outs), F32),
        in_specs=[pl.BlockSpec(memory_space=pl.ANY)] * 2,
        out_specs=pl.BlockSpec(memory_space=VMEM),
        scratch_shapes=[
            VMEM(keep.shape, F32),
            buf(pairs, quarters, depth),
            buf(pairs, 2, half),
            buf(pairs, 2, rest),
            buf(pairs, 2, half),
            buf(pairs, 2, rest),
            buf(pairs, half),
            buf(pairs, rest),
            buf(pairs, half),
            buf(pairs, rest),
            buf(pairs, depth),
            buf(pairs, depth),
            pltpu.SemaphoreType.DMA((6, pairs)),
            pltpu.SemaphoreType.DMA((6, pairs)),
            pltpu.SemaphoreType.DMA,
        ],
        compiler_params=pltpu.CompilerParams(
            collective_id=0, has_side_effects=True, vmem_limit_bytes=LIMIT
        ),
    )(keep, give)


def shards(features, cotangent, w_point, w_rate_a, w_rate_b, w_rate_c, w_proj, bucket_slot):
    n = features.shape[1]
    chans = features.shape[3]
    outs = w_point.shape[1]
    pix = n * n
    f = features.reshape(pix, chans)
    cot = cotangent.reshape(pix, outs)
    replicas = lax.axis_size("dp")
    nslice = bucket_slot.shape[0]
    cap = nslice // replicas + 1
    g01, ft, pb = forward(n, f, w_rate_c, w_rate_b, w_rate_a, w_point, cot, w_proj)
    keep, give = grads(n, cap, replicas // 2, bucket_slot, g01, ft, pb)
    shape = (replicas // 2, 4, cap * (SROWS // 4), outs)
    total = reduce_scatter(keep.reshape(shape), give.reshape(shape))
    return total.reshape(cap, SROWS // 4 * outs)


def solution(mesh):
    placed = (
        P("dp", "row", "col", None),
        P("dp", "row", "col", None),
        P(),
        P(),
        P(),
        P(),
        P(),
        P(),
    )
    return jax.shard_map(
        shards, mesh=mesh, in_specs=placed, out_specs=P("dp", ("row", "col")), check_vma=False
    )
```

time: 124 us -> 98.1 us (0.79)
  waiting for transfers between devices: 26.6 us -> 0 us
  Pallas kernels: 87.1 us -> 96 us
  starting transfers between devices: 5.95 us -> 0 us
  local copies, waits for them, and re-layouts: 3.57 us -> 1.81 us
    ppermute x6 -> x0, waiting for transfers between devices: 26.6 us -> none  [the longest x1 17.7 us: shards(): d = lax.ppermute(d, ('row', 'col'), cross)]
    pallas_call x1, Pallas kernels: 18.4 us -> 40.2 us  [forward(): pl.pallas_call(functools.partial(forward_kernel, n), grid=(10,), out_shap...]
    ppermute x6 -> x0, starting transfers between devices: 5.95 us -> none  [the longest x1 2.09 us: shards(): h = lax.ppermute(h, 'col', swap)]
    pallas_call x1 -> x0, Pallas kernels: 5.15 us -> none  [middle(): pl.pallas_call(functools.partial(middle_kernel, n), out_shape=[jax.ShapeD...]
    pallas_call x1, Pallas kernels: 43.7 us -> 38.8 us  [reduce_scatter(): pl.pallas_call(functools.partial(reduce_kernel, pairs, half), out_shape=j...]
    pallas_call x1, Pallas kernels: 19.9 us -> 16.9 us  [grads(): pl.pallas_call(functools.partial(grads_kernel, n, cap), out_shape=[jax.Sh...]
    unnamed x12 -> x0, local copies, waits for them, and re-layouts: 1.76 us -> none
  transfers between devices with their start and end apart: 6 -> 0, of which waited for: 4 -> 0; matrix products, arithmetic and copies ran while one was open for 0% -> 0% of each run, Pallas kernels for 0% -> 0%
where the time goes in v2:
time: 98.1 us; the launch traced here: 97.8 us
  Pallas kernels  96 us (98%)
  local copies, waits for them, and re-layouts  1.81 us (2%)
    pallas_call x1, Pallas kernels, forward(): pl.pallas_call(functools.partial(forward_kernel, n), grid=(10,), out_shap...  40.2 us
    pallas_call x1, Pallas kernels, reduce_scatter(): pl.pallas_call(functools.partial(reduce_kernel, pairs, half), out_shape=j...  38.8 us
    pallas_call x1, Pallas kernels, grads(): pl.pallas_call(functools.partial(grads_kernel, n, cap), out_shape=[jax.Sh...  16.9 us

profile of v2, /device:TPU:1, one launch (start us, length us, event | category | flops | bytes accessed | tf_op | source)
XLA Modules:
  0.0 97.8 jit_solution(13559443214287379679)
XLA Ops:
  0.0 40.2 %shard_map.82 = (f32[2048,256]{1,0:T(8,128)}, bf16[1024,576]{1,0:T(8,128)(2,1)}, bf16[1440,768]{1,0:T(8,128)(2,1)}) custom-call(bf16[576,1024]{1,0:T(8,128)(2,1)} %bitcast.6, bf16[3,3,1024,256]{3,2,1,0:T(8,128)(2,1)} %wc_ref.1, bf16[3,3,1024,256]{3,2,1,0:T(8,128)(2,1)} %wb_ref.1, bf16[3,3,1024,256]{3,2,1,0:T(8,128)(2,1)} %wa_ref.1, ...), custom_call_target="tpu_custom_call" | custom-call | tf_op jit(solution)/shard_map/pallas_call | solution.py:195
  40.2 16.9 %shard_map.83 = (f32[4,4,23,16,256]{4,3,2,1,0:T(8,128)}, bf16[4,4,23,16,256]{4,3,2,1,0:T(8,128)(2,1)}) custom-call(s32[176]{0:T(256)} %bs_ref.1, f32[2048,256]{1,0:T(8,128)} %get-tuple-element.10.g01_ref, bf16[1024,576]{1,0:T(8,128)(2,1)} %get-tuple-element.11.ft_ref, bf16[1440,768]{1,0:T(8,128)(2,1)} %get-tuple-element.12.pb_ref), custom_call_target="tpu_custom_call" | custom-call | tf_op jit(solution)/shard_map/pallas_call | solution.py:264
  57.2 38.8 %shard_map.84 = f32[368,256]{1,0:T(8,128)} custom-call(f32[4,4,368,256]{3,2,1,0:T(8,128)} %bitcast.4, bf16[4,4,368,256]{3,2,1,0:T(8,128)(2,1)} %bitcast.5), custom_call_target="tpu_custom_call" | custom-call | tf_op jit(solution)/shard_map/pallas_call | solution.py:365
  96.0 1.8 %reshape.19 = f32[23,4096]{1,0:T(8,128)} reshape(f32[368,256]{1,0:T(8,128)} %shard_map.84) | data formatting | bytes 753664 | tf_op jit(solution)/shard_map/reshape | solution.py:407
